TPU v7x, 128 devices: a whole 4x4x4 slice. The times are simulated.
128 devices in a mesh: row: 16 (over y_lo, z, core), col: 8 (over y_hi, x).
Axes of the slice: x: 4, y: 4 (y_hi: 2, y_lo: 2; y = y_hi * 2 + y_lo), z: 4, core: 2. Of those that a mesh axis runs over, the one named last changes fastest.
Arguments:
- tokens: bfloat16 [1024, 6144], P('col', 'row'), may hold values from -6 to 6
- weight_in: bfloat16 [6144, 24576], P('row', 'col'), may hold values from -0.078125 to 0.078125
- weight_out: bfloat16 [24576, 6144], P('col', 'row'), may hold values from -0.078125 to 0.078125
- upstream: bfloat16 [1024, 6144], P('col', 'row'), may hold values from -6 to 6
Outputs:
- grad_tokens: bfloat16 [1024, 6144], P('col', 'row')
- grad_in: bfloat16 [6144, 24576], P('row', 'col')
- grad_out: bfloat16 [24576, 6144], P('col', 'row')
All inputs are finite; a program needn't handle non-finite values.
Results may differ from a plain program's by a relative error of at most 0.005.
Values may be sent and summed in bfloat16 or wider, within the bound.
A program may use at most 128 MiB of HBM per device.

v0:
```python
import jax
import jax.numpy as jnp
from jax import lax
from jax.sharding import PartitionSpec as P

coef = 0.7978845608
cubic = 0.044715


def activate(hidden, back):
    inner = coef * (hidden + cubic * hidden * hidden * hidden)
    tangent = jnp.tanh(inner)
    value = 0.5 * hidden * (1.0 + tangent)
    slope = 0.5 * (1.0 + tangent) + 0.5 * hidden * (1.0 - tangent * tangent) * coef * (
        1.0 + 3.0 * cubic * hidden * hidden
    )
    return (value.astype(jnp.bfloat16), (back * slope).astype(jnp.bfloat16))


def contract_last(left, right):
    return lax.dot_general(
        left, right, (((1,), (1,)), ((), ())), preferred_element_type=jnp.float32
    )


def contract_first(left, right):
    return lax.dot_general(
        left, right, (((0,), (0,)), ((), ())), preferred_element_type=jnp.float32
    )


def shards(tokens, weight_in, weight_out, upstream):
    tok_all, cot_all = (
        lax.all_gather(tokens, "col", axis=0, tiled=True),
        lax.all_gather(upstream, "col", axis=0, tiled=True),
    )
    width_hid = weight_in.shape[1]
    sums = lax.psum_scatter(
        jnp.concatenate(
            [
                jnp.dot(tok_all, weight_in, preferred_element_type=jnp.float32),
                contract_last(cot_all, weight_out),
            ],
            axis=1,
        ),
        "row",
        scatter_dimension=0,
        tiled=True,
    )
    hidden_local = sums[:, :width_hid]
    back_local = sums[:, width_hid:]
    act_local, grad_local = activate(hidden_local, back_local)
    act_all, grad_all = (
        lax.all_gather(act_local, "row", axis=0, tiled=True),
        lax.all_gather(grad_local, "row", axis=0, tiled=True),
    )
    grad_in = contract_first(tok_all, grad_all).astype(jnp.bfloat16)
    grad_out = contract_first(act_all, cot_all).astype(jnp.bfloat16)
    grad_tokens = lax.psum_scatter(
        contract_last(grad_all, weight_in), "col", scatter_dimension=0, tiled=True
    ).astype(jnp.bfloat16)
    return (grad_tokens, grad_in, grad_out)


def solution(mesh):
    placed = (P("col", "row"), P("row", "col"), P("col", "row"), P("col", "row"))
    return jax.shard_map(
        shards,
        mesh=mesh,
        in_specs=placed,
        out_specs=(P("col", "row"), P("row", "col"), P("col", "row")),
        check_vma=False,
    )
```

profile of v0, /device:TPU:0, one launch (start us, length us, event | category | flops | bytes accessed | tf_op | source)
XLA Modules:
  0.0 416.0 jit_solution(14746245070475281897)
XLA Ops:
  7.2 0.0 copy-start
  7.2 0.0 reduce-scatter.3.cloned.1.call-start
  7.2 36.7 %all_gather.12 = bf16[1024,384]{1,0:T(8,128)(2,1)S(1)} all-gather(bf16[128,384]{1,0:T(8,128)(2,1)} %param.4), channel_id=1, replica_groups=mesh['row'=16,'col'=8] {'col'}, dimensions={0}, use_global_device_ids=true | all-gather | bytes 884736 | tf_op jit(solution)/shard_map/all_gather | solution.py:34
  43.9 35.8 %all_gather.13 = bf16[1024,384]{1,0:T(8,128)(2,1)S(1)} all-gather(bf16[128,384]{1,0:T(8,128)(2,1)} %param.7), channel_id=1, replica_groups=mesh['row'=16,'col'=8] {'col'}, dimensions={0}, use_global_device_ids=true | all-gather | bytes 884736 | tf_op jit(solution)/shard_map/all_gather | solution.py:35
  79.7 0.0 copy-start.1
  79.7 5.4 %fusion.9 = f32[1024,3072]{1,0:T(8,128)S(1)} fusion(bf16[1024,384]{1,0:T(8,128)(2,1)S(1)} %all_gather.13, bf16[3072,384]{1,0:T(8,128)(2,1)} %param.6), kind=kOutput, calls=%fused_computation.15 | convolution fusion | flops 2415919104 | bytes 15728640 | tf_op jit(solution)/shard_map/dot_general | solution.py:21
  85.2 0.0 copy-done.1
  85.2 0.0 copy-done
  85.2 3.4 fusion.8
  88.6 8.7 %pad_maximum_fusion = f32[1024,6144]{1,0:T(8,128)} fusion(f32[1024,3072]{1,0:T(8,128)S(1)} %fusion.9, f32[1024,3072]{1,0:T(8,128)S(1)} %fusion.8), kind=kLoop, calls=%fused_computation | loop fusion | flops 6291456 | bytes 50331648 | tf_op jit(solution)/shard_map/concatenate | solution.py:39
  97.3 0.0 reduce-scatter.3.cloned.1.call-update
  97.4 0.0 all-gather.3.cloned.1.call-start
  97.4 142.9 %reduce-scatter.3.cloned.1.call-done = f32[64,6144]{1,0:T(8,128)} async-done(((f32[1024,6144]{1,0:T(8,128)}), f32[64,6144]{1,0:T(8,128)}) %reduce-scatter.3.cloned.1.call-update) | async-done | bytes 1572880 | tf_op jit(solution)/shard_map/reduce_scatter | solution.py:38
  240.3 2.8 multiply_convert_fusion
  243.0 0.0 all-gather.3.cloned.1.call-update
  243.1 0.0 all-gather.5.cloned.1.call-start
  243.1 0.7 all-gather.5.cloned.1.call-update
  243.8 0.2 reduce-scatter.5.cloned.1.call-start
  244.0 40.1 %all-gather.3.cloned.1.call-done = bf16[1024,3072]{1,0:T(8,128)(2,1)} async-done(((bf16[64,3072]{1,0:T(8,128)(2,1)}), bf16[1024,3072]{1,0:T(8,128)(2,1)}) %all-gather.3.cloned.1.call-update) | async-done | bytes 6291472 | tf_op jit(solution)/shard_map/all_gather | solution.py:55
  284.2 6.7 %fusion.10 = f32[1024,384]{1,0:T(8,128)} fusion(bf16[1024,3072]{1,0:T(8,128)(2,1)} %all-gather.3.cloned.1.call-done, bf16[384,3072]{1,0:T(8,128)(2,1)S(1)} %copy-done), kind=kOutput, calls=%fused_computation.16 | convolution fusion | flops 2415919104 | bytes 10223616 | tf_op jit(solution)/shard_map/dot_general | solution.py:21
  290.8 0.0 reduce-scatter.5.cloned.1.call-update
  290.9 7.7 %fusion = bf16[384,3072]{0,1:T(8,128)(2,1)} fusion(bf16[1024,3072]{1,0:T(8,128)(2,1)} %all-gather.3.cloned.1.call-done, bf16[1024,384]{1,0:T(8,128)(2,1)S(1)} %all_gather.12), kind=kOutput, calls=%fused_computation.3 | convolution fusion | flops 2417098752 | bytes 9437184 | tf_op jit(solution)/shard_map/dot_general | solution.py:27
  298.5 0.0 copy-start.2
  298.5 4.3 %copy.7 = bf16[384,3072]{1,0:T(8,128)(2,1)} copy(bf16[384,3072]{0,1:T(8,128)(2,1)} %fusion) | data formatting | bytes 4718592
  302.9 26.3 %all-gather.5.cloned.1.call-done = bf16[1024,3072]{1,0:T(8,128)(2,1)} async-done(((bf16[64,3072]{1,0:T(8,128)(2,1)}), bf16[1024,3072]{1,0:T(8,128)(2,1)}) %all-gather.5.cloned.1.call-update) | async-done | bytes 6291472 | tf_op jit(solution)/shard_map/all_gather | solution.py:54
  329.2 0.0 copy-done.2
  329.2 7.7 %convolution_convert_fusion = bf16[3072,384]{1,0:T(8,128)(2,1)} fusion(bf16[1024,3072]{1,0:T(8,128)(2,1)} %all-gather.5.cloned.1.call-done, bf16[1024,384]{1,0:T(8,128)(2,1)S(1)} %copy-done.2), kind=kOutput, calls=%fused_computation.1 | convolution fusion | flops 2417098752 | bytes 9437184 | tf_op jit(solution)/shard_map/dot_general | solution.py:27
  336.8 71.0 %reduce-scatter.5.cloned.1.call-done = f32[128,384]{1,0:T(8,128)} async-done(((f32[1024,384]{1,0:T(8,128)}), f32[128,384]{1,0:T(8,128)}) %reduce-scatter.5.cloned.1.call-update) | async-done | bytes 196624 | tf_op jit(solution)/shard_map/reduce_scatter | solution.py:59
  407.9 1.6 convert_element_type.19
Async XLA Ops:
  7.2 78.0 %copy-start = (bf16[384,3072]{1,0:T(8,128)(2,1)S(1)}, bf16[384,3072]{1,0:T(8,128)(2,1)}, u32[]{:S(2)}) copy-start(bf16[384,3072]{1,0:T(8,128)(2,1)} %param.5) | copy-start | bytes 7077892
  7.2 233.1 %reduce-scatter.3.cloned.1.call-start = ((), (), s32[]{:S(2)}) async-start(), calls=%async_computation.2 | async-start | bytes 26738688 | tf_op jit(solution)/shard_map/reduce_scatter | solution.py:38
  79.7 5.4 %copy-start.1 = (bf16[1024,384]{1,0:T(8,128)(2,1)}, bf16[1024,384]{1,0:T(8,128)(2,1)S(1)}, u32[]{:S(2)}) copy-start(bf16[1024,384]{1,0:T(8,128)(2,1)S(1)} %all_gather.13) | copy-start | bytes 2359300
  97.4 186.8 %all-gather.3.cloned.1.call-start = ((), (), s32[]{:S(2)}) async-start(), calls=%async_computation.3 | async-start | bytes 6684672 | tf_op jit(solution)/shard_map/all_gather | solution.py:55
  243.1 86.1 %all-gather.5.cloned.1.call-start = ((), (), s32[]{:S(2)}) async-start(), calls=%async_computation.5 | async-start | bytes 6684672 | tf_op jit(solution)/shard_map/all_gather | solution.py:54
  243.8 164.1 %reduce-scatter.5.cloned.1.call-start = ((), (), s32[]{:S(2)}) async-start(), calls=%async_computation.4 | async-start | bytes 1769472 | tf_op jit(solution)/shard_map/reduce_scatter | solution.py:59
  298.5 30.6 %copy-start.2 = (bf16[1024,384]{1,0:T(8,128)(2,1)S(1)}, bf16[1024,384]{1,0:T(8,128)(2,1)}, u32[]{:S(2)}) copy-start(bf16[1024,384]{1,0:T(8,128)(2,1)} %copy-done.1) | copy-start | bytes 2359300
Sparse Core Ops, SparseCore 0:
  97.5 142.7 reduce-scatter.2
  243.2 40.9 all-gather.2
  285.9 43.2 all-gather.4
  332.8 75.0 reduce-scatter.4
where the time goes:
time: 416 us
  waiting for transfers between devices  281 us (68%)
  blocking collectives  72.5 us (17%)
  matrix products  30.9 us (7%)
  between operations  13.8 us (3%)
  other arithmetic  13.1 us (3%)
  local copies, waits for them, and re-layouts  4.37 us (1%)
    reduce_scatter x1, waiting for transfers between devices, shards(): lax.psum_scatter(jnp.concatenate([jnp.dot(tok_all, weight_in, preferred_e...  143 us
    reduce_scatter x1, waiting for transfers between devices, shards(): lax.psum_scatter(contract_last(grad_all, weight_in), 'col', scatter_dimen...  71 us
    all_gather x1, waiting for transfers between devices, shards(): lax.all_gather(grad_local, 'row', axis=0, tiled=True)  40.1 us
    all_gather x1, blocking collectives, shards(): lax.all_gather(tokens, 'col', axis=0, tiled=True)  36.7 us
    all_gather x1, blocking collectives, shards(): lax.all_gather(upstream, 'col', axis=0, tiled=True)  35.8 us
    all_gather x1, waiting for transfers between devices, shards(): lax.all_gather(act_local, 'row', axis=0, tiled=True)  26.3 us
    dot_general x2, matrix products, contract_first(): lax.dot_general(left, right, (((0,), (0,)), ((), ())), preferred_element_...  15.3 us
    dot_general x2, matrix products, contract_last(): lax.dot_general(left, right, (((1,), (1,)), ((), ())), preferred_element_...  12.1 us
  transfers between devices with their start and end apart: 4, of which 4 were waited for; matrix products, arithmetic and copies ran while one was open for 6% of the time, Pallas kernels for 0%

commit v1 on v0

v1 whole, which is shorter than its diff:
```python
import jax
import jax.numpy as jnp
from jax import lax
from jax.experimental import pallas as pl
from jax.experimental.pallas import tpu as pltpu
from jax.sharding import PartitionSpec as P

coef = 0.7978845608
cubic = 0.044715
BF = jnp.bfloat16
F32 = jnp.float32
MESH = pl.DeviceIdType.MESH

N = 8
TB = 128
DH = 384
DC = 768
FH = 1536
FP = 512
FQ = 1024
TILE = 512


def activate(hidden, back):
    inner = coef * (hidden + cubic * hidden * hidden * hidden)
    tangent = jnp.tanh(inner)
    value = 0.5 * hidden * (1.0 + tangent)
    slope = 0.5 * (1.0 + tangent) + 0.5 * hidden * (1.0 - tangent * tangent) * coef * (
        1.0 + 3.0 * cubic * hidden * hidden
    )
    return value.astype(BF), (back * slope).astype(BF)


def dot(left, right):
    return jnp.dot(left, right, preferred_element_type=F32)


def dot_nt(left, right):
    return lax.dot_general(
        left, right, (((1,), (1,)), ((), ())), preferred_element_type=F32
    )


def kernel(
    tok_ref, win_ref, wout_ref, up_ref,
    gtok_ref, gin_ref, gout_ref,
    wi, wo, tk, pp, yp, s1, rzp, szp, gp, pq, rzq, szq, kq, syq, yq, gq,
    acci, acco, sti, sto, down, doth, dsib, dr, yhs, yhr, tkt,
    ss, rs, ls, ws, wr, os, orr, hs, hr,
):
    r, c = lax.axis_index("row"), lax.axis_index("col")
    yl, z, k = r // 8, (r // 2) % 4, r % 2
    yh, x = c // 4, c % 4
    zr, zl, z2 = (z + 1) % 4, (z + 3) % 4, (z + 2) % 4

    def at_row(yl_, z_, k_):
        return (yl_ * 8 + z_ * 2 + k_, c)

    def at_col(yh_, x_):
        return (r, yh_ * 4 + x_)

    sib, ypart = at_row(yl, z, 1 - k), at_row(1 - yl, z, k)
    right, left = at_row(yl, zr, k), at_row(yl, zl, k)
    yhp = at_col(1 - yh, x)
    xr, xl, xx = at_col(yh, (x + 1) % 4), at_col(yh, (x + 3) % 4), at_col(yh, (x + 2) % 4)

    def rc(src, dst, send, recv, dev):
        return pltpu.make_async_remote_copy(
            src_ref=src, dst_ref=dst, send_sem=send, recv_sem=recv,
            device_id=dev, device_id_type=MESH,
        )

    def rows(i, size):
        return pl.ds(pl.multiple_of(i * size, size), size)

    def msg(n, i):
        own_p = pl.ds(pl.multiple_of(yl * 64 + z * 16, 16), 16)
        left_p = pl.ds(pl.multiple_of(yl * 64 + zl * 16, 16), 16)
        right_p = pl.ds(pl.multiple_of(yl * 64 + zr * 16, 16), 16)
        own_q = pl.ds(pl.multiple_of(z * 32 + yl * 16, 16), 16)
        if i == 0:
            src, dst, dev = pp.at[n, :, rows(1 - yl, 64)], yp.at[n], ypart
        elif i == 1:
            src, dst, dev = s1.at[n, 0, rows(z2, 16)], rzp.at[n, 0], right
        elif i == 2:
            src, dst, dev = s1.at[n, 1, rows(zr, 16)], rzp.at[n, 1], right
        elif i == 3:
            src, dst, dev = s1.at[n, 1, rows(z2, 16)], rzp.at[n, 2], left
        elif i == 4:
            src, dst, dev = s1.at[n, 0, rows(zl, 16)], rzp.at[n, 3], left
        elif i == 5:
            src, dst, dev = szp.at[n, 0], rzp.at[n, 4], right
        elif i == 6:
            src, dst, dev = szp.at[n, 1], rzp.at[n, 5], left
        elif i in (7, 8):
            src = dst = gp.at[n, :, own_p]
            dev = right if i == 7 else left
        elif i == 9:
            src = dst = gp.at[n, 0, left_p]
            dev = right
        elif i == 10:
            src = dst = gp.at[n, 1, right_p]
            dev = left
        elif i == 11:
            src = dst = gp.at[n, :, rows(yl, 64)]
            dev = ypart
        elif i == 12:
            src, dst, dev = syq.at[n], yq.at[n], ypart
        elif i == 13:
            src, dst, dev = pq.at[n, 0, rows(z2, 32)], rzq.at[n, 0], right
        elif i == 14:
            src, dst, dev = pq.at[n, 1, rows(zr, 32)], rzq.at[n, 1], right
        elif i == 15:
            src, dst, dev = pq.at[n, 1, rows(z2, 32)], rzq.at[n, 2], left
        elif i == 16:
            src, dst, dev = pq.at[n, 0, rows(zl, 32)], rzq.at[n, 3], left
        elif i == 17:
            src, dst, dev = szq.at[n, 0], rzq.at[n, 4], right
        elif i == 18:
            src, dst, dev = szq.at[n, 1], rzq.at[n, 5], left
        elif i == 19:
            src = dst = gq.at[n, :, own_q]
            dev = ypart
        elif i in (20, 21):
            src = dst = gq.at[n, :, rows(z, 32)]
            dev = right if i == 20 else left
        elif i == 22:
            src = dst = gq.at[n, 0, rows(zl, 32)]
            dev = right
        elif i == 23:
            src = dst = gq.at[n, 1, rows(zr, 32)]
            dev = left
        elif i == 24:
            src, dst, dev = doth.at[n], dsib.at[n], sib
        elif i == 25:
            m = (n + 2) % 3
            dx = 1 + 2 * m - 3 * (m // 2)
            src, dst, dev = down.at[n], dr.at[n], at_col(yh, (x + dx) % 4)
        elif i == 27:
            src = dst = tk.at[n, :, :, own_d]
            dev = sib
        return rc(src, dst, ss.at[n, i], rs.at[n, i], dev)

    own_d = pl.ds(pl.multiple_of(k * DH, DH), DH)
    oth_d = pl.ds(pl.multiple_of((1 - k) * DH, DH), DH)
    own_f = pl.ds(pl.multiple_of(k * FH, FH), FH)
    oth_f = pl.ds(pl.multiple_of((1 - k) * FH, FH), FH)

    def tok_msg(m):
        dev = {1: xl, 2: xr, 3: xx, 4: xl, 5: xr, 6: xx, 7: yhp}[m]
        src = tk.at[0 if m in (1, 2, 3, 7) else 7, :, :, own_d]
        return rc(src, tk.at[m, :, :, own_d], ss.at[m, 26], rs.at[m, 26], dev)

    w_out = [
        rc(win_ref.at[:, oth_f], wi.at[own_d], ws.at[0], wr.at[0], sib),
        rc(wout_ref.at[oth_f], wo.at[:, own_d], ws.at[1], wr.at[1], sib),
    ]
    w_own = [
        pltpu.make_async_copy(win_ref.at[:, own_f], wi.at[own_d], ls.at[0]),
        pltpu.make_async_copy(wout_ref.at[own_f], wo.at[:, own_d], ls.at[1]),
    ]
    for cp in w_own:
        cp.start()
    tk[0, 0, :, own_d] = tok_ref[...]
    tk[0, 1, :, own_d] = up_ref[...]

    barrier = pltpu.get_barrier_semaphore()
    partners = (sib, ypart, right, left, yhp, xr, xl, xx)
    for dev in partners:
        pl.semaphore_signal(barrier, inc=1, device_id=dev, device_id_type=MESH)
    pl.semaphore_wait(barrier, len(partners))

    msg(0, 27).start()
    tok_msg(7).start()
    for cp in w_out:
        cp.start()
    for m in (1, 2, 3):
        tok_msg(m).start()
    acci[...] = jnp.zeros_like(acci)
    acco[...] = jnp.zeros_like(acco)
    for cp in w_own:
        cp.wait()
    for cp in w_out:
        cp.wait_recv()

    def s0(n):
        msg(n, 27).wait_recv()
        pp[n, 0] = dot(tk[n, 0], wi[:, 0:FP]).astype(BF)
        pp[n, 1] = dot_nt(tk[n, 1], wo[0:FP, :]).astype(BF)
        msg(n, 0).start()
        for j in range(0, FQ, TILE):
            pq[n, 0, :, j : j + TILE] = dot(tk[n, 0], wi[:, FP + j : FP + j + TILE]).astype(BF)
            pq[n, 1, :, j : j + TILE] = dot_nt(tk[n, 1], wo[FP + j : FP + j + TILE, :]).astype(BF)
        for i in (13, 15, 14, 16):
            msg(n, i).start()

    def s1f(n):
        msg(n, 0).wait_recv()
        s1[n] = (pp[n, :, rows(yl, 64)].astype(F32) + yp[n].astype(F32)).astype(BF)
        for i in (1, 3, 2, 4):
            msg(n, i).start()
        msg(n, 13).wait_recv()
        szq[n, 0] = (pq[n, 0, rows(zr, 32)].astype(F32) + rzq[n, 0].astype(F32)).astype(BF)
        msg(n, 17).start()
        msg(n, 15).wait_recv()
        szq[n, 1] = (pq[n, 1, rows(zl, 32)].astype(F32) + rzq[n, 2].astype(F32)).astype(BF)
        msg(n, 18).start()

    def s2(n):
        msg(n, 1).wait_recv()
        szp[n, 0] = (s1[n, 0, rows(zr, 16)].astype(F32) + rzp[n, 0].astype(F32)).astype(BF)
        msg(n, 5).start()
        msg(n, 3).wait_recv()
        szp[n, 1] = (s1[n, 1, rows(zl, 16)].astype(F32) + rzp[n, 2].astype(F32)).astype(BF)
        msg(n, 6).start()
        for i in (14, 16, 17, 18):
            msg(n, i).wait_recv()
        for t, a, b in ((0, 3, 4), (1, 1, 5)):
            for mine in (False, True):
                half = yl if mine else 1 - yl
                here = pl.ds(pl.multiple_of(z * 32 + half * 16, 16), 16)
                total = (
                    pq[n, t, here].astype(F32)
                    + rzq[n, a, rows(half, 16)].astype(F32)
                    + rzq[n, b, rows(half, 16)].astype(F32)
                )
                if mine:
                    kq[n, t] = total
                else:
                    syq[n, t] = total.astype(BF)
        msg(n, 12).start()

    def s3(n):
        for i in (2, 4, 5, 6):
            msg(n, i).wait_recv()
        hidden = s1[n, 0, rows(z, 16)].astype(F32) + rzp[n, 3].astype(F32) + rzp[n, 4].astype(F32)
        back = s1[n, 1, rows(z, 16)].astype(F32) + rzp[n, 1].astype(F32) + rzp[n, 5].astype(F32)
        here = pl.ds(pl.multiple_of(yl * 64 + z * 16, 16), 16)
        gp[n, 0, here], gp[n, 1, here] = activate(hidden, back)
        msg(n, 7).start()
        msg(n, 8).start()
        msg(n, 12).wait_recv()
        here = pl.ds(pl.multiple_of(z * 32 + yl * 16, 16), 16)
        gq[n, 0, here], gq[n, 1, here] = activate(
            kq[n, 0] + yq[n, 0].astype(F32), kq[n, 1] + yq[n, 1].astype(F32)
        )
        msg(n, 19).start()

    def s4(n):
        msg(n, 19).wait_recv()
        msg(n, 20).start()
        msg(n, 21).start()
        msg(n, 7).wait_recv()
        msg(n, 9).start()
        msg(n, 8).wait_recv()
        msg(n, 10).start()

    def s5(n):
        msg(n, 9).wait_recv()
        msg(n, 10).wait_recv()
        msg(n, 11).start()
        msg(n, 20).wait_recv()
        msg(n, 22).start()
        msg(n, 21).wait_recv()
        msg(n, 23).start()

    def s6_wait(n):
        for i in (11, 22, 23):
            msg(n, i).wait_recv()

    def cols(t, n):
        ref = gp
        yield 0, ref[n, t]
        for j in range(0, FQ, TILE):
            yield FP + j, gq[n, t, :, j : j + TILE]

    def s6a(n):
        tkt[...] = tk[n, 0].T
        for j, g in cols(1, n):
            acci[:, j : j + TILE] += dot(tkt[...], g)

    def s6b(n):
        for half, ref in ((oth_d, doth), (own_d, down)):
            ref[n] = dot_nt(gp[n, 1], wi[half, 0:FP]) + dot_nt(gq[n, 1], wi[half, FP:FH])
            if ref is doth:
                msg(n, 24).start()
        for j, a in cols(0, n):
            acco[j : j + TILE, :] += dot(a.T, tk[n, 1])

    def s7(n):
        msg(n, 24).wait_recv()
        down[n] += dsib[n]

    def step(n, _):
        @pl.when(n >= 1)
        def _():
            s3(n - 1)

        @pl.when(n < N)
        def _():
            s0(n)
            s1f(n)

        @pl.when(n >= 1)
        def _():
            s4(n - 1)

        @pl.when(n == 0)
        def _():
            tok_msg(7).wait_recv()
            for m in (4, 5, 6):
                tok_msg(m).start()
            msg(7, 27).start()

        for m in range(1, 7):

            @pl.when(n == m - 1)
            def _():
                tok_msg(m).wait_recv()
                msg(m, 27).start()

        @pl.when(n >= 2)
        def _():
            s6_wait(n - 2)
            s6a(n - 2)

        @pl.when(n < N)
        def _():
            s2(n)

        @pl.when(n >= 1)
        def _():
            s5(n - 1)

        @pl.when(n >= 2)
        def _():
            s6b(n - 2)

        @pl.when(n >= 3)
        def _():
            s7(n - 3)

        @pl.when(n >= 4)
        def _():
            msg(n - 3, 25).start()

        return 0

    lax.fori_loop(0, N + 1, step, 0)

    last = N - 1
    s6_wait(last)
    for half, ref in ((oth_d, doth), (own_d, down)):
        ref[last] = dot_nt(gp[last, 1], wi[half, 0:FP]) + dot_nt(gq[last, 1], wi[half, FP:FH])
        if ref is doth:
            msg(last, 24).start()
    s7(last - 1)
    msg(last - 1, 25).start()
    tkt[...] = tk[last, 0].T
    outs = []
    for i, (j, g) in enumerate(cols(1, last)):
        there = pl.ds(pl.multiple_of(k * FH + j, TILE), TILE)
        for mine, half in ((False, oth_d), (True, own_d)):
            sti[half, j : j + TILE] = (acci[half, j : j + TILE] + dot(tkt[half, :], g)).astype(BF)
            src, dst = sti.at[half, j : j + TILE], gin_ref.at[:, there]
            if mine:
                cp = pltpu.make_async_copy(src, dst, ls.at[2 + i])
            else:
                cp = rc(src, dst, os.at[i], orr.at[i], sib)
            cp.start()
            outs.append(cp)
    s7(last)
    for m in (4, 5, 6):
        msg(m, 25).wait_recv()
    yhs[...] = (down[last] + dr[4] + dr[5] + dr[6]).astype(BF)
    yh_msg = rc(yhs, yhr, hs.at[0], hr.at[0], yhp)
    yh_msg.start()
    for i, (j, a) in enumerate(cols(0, last)):
        there = pl.ds(pl.multiple_of(k * FH + j, TILE), TILE)
        at = a.T
        for mine, half in ((False, oth_d), (True, own_d)):
            sto[j : j + TILE, half] = (acco[j : j + TILE, half] + dot(at, tk[last, 1, :, half])).astype(BF)
            src, dst = sto.at[j : j + TILE, half], gout_ref.at[there]
            if mine:
                cp = pltpu.make_async_copy(src, dst, ls.at[5 + i])
            else:
                cp = rc(src, dst, os.at[3 + i], orr.at[3 + i], sib)
            cp.start()
            outs.append(cp)
    for m in (1, 2, 3):
        msg(m, 25).wait_recv()
    yh_msg.wait()
    gtok_ref[...] = (down[0] + dr[1] + dr[2] + dr[3] + yhr[...].astype(F32)).astype(BF)
    for cp in outs:
        cp.wait()

    def drain(n, _):
        for i in list(range(25)) + [27]:
            msg(n, i).wait_send()

        @pl.when((n >= 1) & (n < last))
        def _():
            msg(n, 25).wait_send()

        return 0

    lax.fori_loop(0, N, drain, 0)
    for m in range(1, 8):
        tok_msg(m).wait_send()
    for cp in w_out:
        cp.wait_send()


def shards(tokens, weight_in, weight_out, upstream):
    vm = lambda *shape, dtype=BF: pltpu.VMEM(shape, dtype)
    dma = lambda *shape: pltpu.SemaphoreType.DMA(shape)
    vmem, hbm = pl.BlockSpec(memory_space=pltpu.VMEM), pl.BlockSpec(memory_space=pl.ANY)
    return pl.pallas_call(
        kernel,
        out_shape=(
            jax.ShapeDtypeStruct((TB, DH), BF),
            jax.ShapeDtypeStruct((DH, 2 * FH), BF),
            jax.ShapeDtypeStruct((2 * FH, DH), BF),
        ),
        in_specs=[vmem, hbm, hbm, vmem],
        out_specs=(vmem, hbm, hbm),
        scratch_shapes=[
            vm(DC, FH), vm(FH, DC), vm(N, 2, TB, DC),
            vm(N, 2, TB, FP), vm(N, 2, 64, FP), vm(N, 2, 64, FP), vm(N, 6, 16, FP), vm(N, 2, 16, FP), vm(N, 2, TB, FP),
            vm(N, 2, TB, FQ), vm(N, 6, 32, FQ), vm(N, 2, 32, FQ), vm(N, 2, 16, FQ, dtype=F32), vm(N, 2, 16, FQ), vm(N, 2, 16, FQ), vm(N, 2, TB, FQ),
            vm(DC, FH, dtype=F32), vm(FH, DC, dtype=F32), vm(DC, FH), vm(FH, DC),
            vm(N, TB, DH, dtype=F32), vm(N, TB, DH, dtype=F32), vm(N, TB, DH, dtype=F32), vm(N, TB, DH, dtype=F32),
            vm(TB, DH), vm(TB, DH), vm(DC, TB),
            dma(N, 28), dma(N, 28), dma(8), dma(2), dma(2), dma(6), dma(6), dma(1), dma(1),
        ],
        compiler_params=pltpu.CompilerParams(
            collective_id=0, has_side_effects=True, vmem_limit_bytes=62 << 20
        ),
    )(tokens, weight_in, weight_out, upstream)


def solution(mesh):
    placed = (P("col", "row"), P("row", "col"), P("col", "row"), P("col", "row"))
    return jax.shard_map(
        shards,
        mesh=mesh,
        in_specs=placed,
        out_specs=(P("col", "row"), P("row", "col"), P("col", "row")),
        check_vma=False,
    )
```

time: 416 us -> 159 us (0.38)
  waiting for transfers between devices: 281 us -> 0 us
  Pallas kernels: 0 us -> 151 us
  blocking collectives: 72.5 us -> 0 us
  matrix products: 30.9 us -> 0 us
  between operations: 13.8 us -> 0.64 us
  other arithmetic: 13.1 us -> 0 us
    reduce_scatter x2 -> x0, waiting for transfers between devices: 214 us -> none  [the longest x1 143 us: shards(): lax.psum_scatter(jnp.concatenate([jnp.dot(tok_all, weight_in, preferred_e...]
    pallas_call x0 -> x1, Pallas kernels: none -> 151 us  [shards(): pl.pallas_call(kernel, out_shape=(jax.ShapeDtypeStruct((TB, DH), BF), jax...]
    all_gather x2 -> x0, blocking collectives: 72.5 us -> none  [the longest x1 36.7 us: shards(): lax.all_gather(tokens, 'col', axis=0, tiled=True)]
    all_gather x2 -> x0, waiting for transfers between devices: 66.4 us -> none  [the longest x1 40.1 us: shards(): lax.all_gather(grad_local, 'row', axis=0, tiled=True)]
    dot_general x5 -> x0, matrix products: 30.9 us -> none  [the longest x2 15.3 us: contract_first(): lax.dot_general(left, right, (((0,), (0,)), ((), ())), preferred_element_...]
    concatenate x1 -> x0, other arithmetic: 8.72 us -> none  [shards(): jnp.concatenate([jnp.dot(tok_all, weight_in, preferred_element_type=jnp.f...]
    convert_element_type x2 -> x0, other arithmetic: 4.36 us -> none  [the longest x1 2.78 us: activate(): return (value.astype(jnp.bfloat16), (back * slope).astype(jnp.bfloat16))]
  transfers between devices with their start and end apart: 4 -> 0, of which waited for: 4 -> 0; matrix products, arithmetic and copies ran while one was open for 6% -> 0% of each run, Pallas kernels for 0% -> 0%
where the time goes in v1:
time: 159 us; the launch traced here: 158 us
  Pallas kernels  151 us (95%)
  local copies, waits for them, and re-layouts  6.32 us (4%)
    pallas_call x1, Pallas kernels, shards(): pl.pallas_call(kernel, out_shape=(jax.ShapeDtypeStruct((TB, DH), BF), jax...  151 us
    unnamed x5, local copies, waits for them, and re-layouts  6.32 us

profile of v1, /device:TPU:0, one launch (start us, length us, event | category | flops | bytes accessed | tf_op | source)
XLA Modules:
  0.0 157.8 jit_solution(8050002038174425870)
XLA Ops:
  0.6 150.9 %shard_map.67 = (bf16[128,384]{1,0:T(8,128)(2,1)}, bf16[384,3072]{1,0:T(8,128)(2,1)}, bf16[3072,384]{1,0:T(8,128)(2,1)}) custom-call(bf16[128,384]{1,0:T(8,128)(2,1)} %tok_ref.1, bf16[384,3072]{1,0:T(8,128)(2,1)} %win_ref.1, bf16[3072,384]{1,0:T(8,128)(2,1)} %wout_ref.1, bf16[128,384]{1,0:T(8,128)(2,1)} %up_ref.1), custom_call_target="tpu_custom_call" | custom-call | tf_op jit(solution)/shard_map/pallas_call | solution.py:418
  151.5 1.5 copy.10
  153.1 0.0 copy-start
  153.1 3.4 %copy.11 = bf16[384,3072]{1,0:T(8,128)(2,1)} copy(bf16[384,3072]{1,0:T(8,128)(2,1)} %get-tuple-element.7) | data formatting | bytes 4718592
  156.4 0.0 copy-done
  156.4 1.4 copy.12
Async XLA Ops:
  153.1 3.4 %copy-start = (bf16[3072,384]{1,0:T(8,128)(2,1)S(1)}, bf16[3072,384]{1,0:T(8,128)(2,1)}, u32[]{:S(2)}) copy-start(bf16[3072,384]{1,0:T(8,128)(2,1)} %get-tuple-element.8) | copy-start | bytes 7077892

commit v2 on v1

v2 whole, which is shorter than its diff:
```python
import jax
import jax.numpy as jnp
from jax import lax
from jax.experimental import pallas as pl
from jax.experimental.pallas import tpu as pltpu
from jax.sharding import PartitionSpec as P

coef = 0.7978845608
cubic = 0.044715
BF = jnp.bfloat16
F32 = jnp.float32
MESH = pl.DeviceIdType.MESH

N = 8
TB = 128
DH = 384
DC = 768
FH = 1536
FP = 640
FQ = 896
RECV = {0: 0, 1: 1, 3: 2, 2: 3, 4: 3, 5: 3, 6: 3, 7: 4, 8: 5, 9: 6, 10: 6, 11: 7}
RECV |= {13: 8, 15: 9, 14: 10, 16: 10, 17: 10, 18: 10, 12: 11, 19: 12, 20: 13, 21: 14, 22: 15, 23: 15, 24: 16}
QT = ((0, 512), (512, FQ - 512))
TILES = ((0, FP),) + tuple((FP + j, size) for j, size in QT)


def activate(hidden, back):
    inner = coef * (hidden + cubic * hidden * hidden * hidden)
    tangent = jnp.tanh(inner)
    value = 0.5 * hidden * (1.0 + tangent)
    slope = 0.5 * (1.0 + tangent) + 0.5 * hidden * (1.0 - tangent * tangent) * coef * (
        1.0 + 3.0 * cubic * hidden * hidden
    )
    return value.astype(BF), (back * slope).astype(BF)


def dot(left, right):
    return jnp.dot(left, right, preferred_element_type=F32)


def dot_nt(left, right):
    return lax.dot_general(
        left, right, (((1,), (1,)), ((), ())), preferred_element_type=F32
    )


def kernel(
    tok_ref, win_ref, wout_ref, up_ref,
    gtok_ref, gin_ref, gout_ref,
    wi, wo, tk, pp, yp, s1, rzp, szp, gp, pq, rzq, szq, kq, syq, yq, gq,
    acci, acco, sti, sto, down, doth, dsib, dr, yhs, yhr, tkt,
    ss, rs, rs25, rs26, rs27, ls, ws, wr, os, orr, hs, hr,
):
    r, c = lax.axis_index("row"), lax.axis_index("col")
    yl, z, k = r // 8, (r // 2) % 4, r % 2
    yh, x = c // 4, c % 4
    zr, zl, z2 = (z + 1) % 4, (z + 3) % 4, (z + 2) % 4

    def at_row(yl_, z_, k_):
        return (yl_ * 8 + z_ * 2 + k_, c)

    def at_col(yh_, x_):
        return (r, yh_ * 4 + x_)

    sib, ypart = at_row(yl, z, 1 - k), at_row(1 - yl, z, k)
    right, left = at_row(yl, zr, k), at_row(yl, zl, k)
    yhp = at_col(1 - yh, x)
    xr, xl, xx = at_col(yh, (x + 1) % 4), at_col(yh, (x + 3) % 4), at_col(yh, (x + 2) % 4)

    def rc(src, dst, send, recv, dev):
        return pltpu.make_async_remote_copy(
            src_ref=src, dst_ref=dst, send_sem=send, recv_sem=recv,
            device_id=dev, device_id_type=MESH,
        )

    def rows(i, size):
        return pl.ds(pl.multiple_of(i * size, size), size)

    def landed(ref, sem):
        pltpu.make_async_copy(ref, ref, sem).wait()

    def msg(n, i):
        own_p = pl.ds(pl.multiple_of(yl * 64 + z * 16, 16), 16)
        left_p = pl.ds(pl.multiple_of(yl * 64 + zl * 16, 16), 16)
        right_p = pl.ds(pl.multiple_of(yl * 64 + zr * 16, 16), 16)
        own_q = pl.ds(pl.multiple_of(z * 32 + yl * 16, 16), 16)
        if i == 0:
            src, dst, dev = pp.at[n, :, rows(1 - yl, 64)], yp.at[n], ypart
        elif i == 1:
            src, dst, dev = s1.at[n, 0, rows(z2, 16)], rzp.at[n, 0], right
        elif i == 2:
            src, dst, dev = s1.at[n, 1, rows(zr, 16)], rzp.at[n, 2], right
        elif i == 3:
            src, dst, dev = s1.at[n, 1, rows(z2, 16)], rzp.at[n, 1], left
        elif i == 4:
            src, dst, dev = s1.at[n, 0, rows(zl, 16)], rzp.at[n, 3], left
        elif i == 5:
            src, dst, dev = szp.at[n, 0], rzp.at[n, 4], right
        elif i == 6:
            src, dst, dev = szp.at[n, 1], rzp.at[n, 5], left
        elif i in (7, 8):
            src = dst = gp.at[n, :, own_p]
            dev = right if i == 7 else left
        elif i == 9:
            src = dst = gp.at[n, 0, left_p]
            dev = right
        elif i == 10:
            src = dst = gp.at[n, 1, right_p]
            dev = left
        elif i == 11:
            src = dst = gp.at[n, :, rows(yl, 64)]
            dev = ypart
        elif i == 12:
            src, dst, dev = syq.at[n], yq.at[n], ypart
        elif i == 13:
            src, dst, dev = pq.at[n, 0, rows(z2, 32)], rzq.at[n, 0], right
        elif i == 14:
            src, dst, dev = pq.at[n, 1, rows(zr, 32)], rzq.at[n, 2], right
        elif i == 15:
            src, dst, dev = pq.at[n, 1, rows(z2, 32)], rzq.at[n, 1], left
        elif i == 16:
            src, dst, dev = pq.at[n, 0, rows(zl, 32)], rzq.at[n, 3], left
        elif i == 17:
            src, dst, dev = szq.at[n, 0], rzq.at[n, 4], right
        elif i == 18:
            src, dst, dev = szq.at[n, 1], rzq.at[n, 5], left
        elif i == 19:
            src = dst = gq.at[n, :, own_q]
            dev = ypart
        elif i in (20, 21):
            src = dst = gq.at[n, :, rows(z, 32)]
            dev = right if i == 20 else left
        elif i == 22:
            src = dst = gq.at[n, 0, rows(zl, 32)]
            dev = right
        elif i == 23:
            src = dst = gq.at[n, 1, rows(zr, 32)]
            dev = left
        elif i == 24:
            src, dst, dev = doth.at[n], dsib.at[n], sib
        elif i == 25:
            m, later = (n - 1) % 3, (n - 1) // 3
            dx = (1 - later) * (1 + 2 * m - 3 * (m // 2)) + later * (2 - m + 3 * (m // 2))
            src, dst, dev = down.at[n], dr.at[n], at_col(yh, (x + dx) % 4)
        elif i == 27:
            src = dst = tk.at[n, :, :, own_d]
            dev = sib
        if i == 27:
            recv = rs27.at[n]
        elif i == 25:
            recv = rs25.at[(n - 1) // 3]
        else:
            recv = rs.at[n % 4, RECV[i]]
        return rc(src, dst, ss.at[N if i == 25 else n], recv, dev)

    own_d = pl.ds(pl.multiple_of(k * DH, DH), DH)
    oth_d = pl.ds(pl.multiple_of((1 - k) * DH, DH), DH)
    own_f = pl.ds(pl.multiple_of(k * FH, FH), FH)
    oth_f = pl.ds(pl.multiple_of((1 - k) * FH, FH), FH)

    def tok_msg(m):
        dev = {1: xl, 2: xr, 3: xx, 4: xx, 5: xl, 6: xr, 7: yhp}[m]
        src = tk.at[0 if m in (1, 2, 3, 7) else 7, :, :, own_d]
        return rc(src, tk.at[m, :, :, own_d], ss.at[N + 1], rs26.at[m], dev)

    w_own, w_out = [], []
    for i, (j, size) in enumerate(TILES):
        mine = pl.ds(pl.multiple_of(k * FH + j, 128), size)
        other = pl.ds(pl.multiple_of((1 - k) * FH + j, 128), size)
        here = pl.ds(j, size)
        w_own += [
            pltpu.make_async_copy(win_ref.at[:, mine], wi.at[own_d, here], ls.at[2 * i]),
            pltpu.make_async_copy(wout_ref.at[mine], wo.at[here, own_d], ls.at[2 * i + 1]),
        ]
        w_out += [
            rc(win_ref.at[:, other], wi.at[own_d, here], ws.at[2 * i], wr.at[2 * i], sib),
            rc(wout_ref.at[other], wo.at[here, own_d], ws.at[2 * i + 1], wr.at[2 * i + 1], sib),
        ]
    w_order = [2, 3, 4, 5, 0, 1]
    for i in w_order:
        w_own[i].start()
    tk[0, 0, :, own_d] = tok_ref[...]
    tk[0, 1, :, own_d] = up_ref[...]

    barrier = pltpu.get_barrier_semaphore()
    partners = (sib, ypart, right, left, yhp, xr, xl, xx)
    for dev in partners:
        pl.semaphore_signal(barrier, inc=1, device_id=dev, device_id_type=MESH)
    pl.semaphore_wait(barrier, len(partners))

    msg(0, 27).start()
    tok_msg(7).start()
    for i in w_order:
        w_out[i].start()
    for m in (1, 2, 3):
        tok_msg(m).start()

    def weights(n, tile):
        @pl.when(n == 0)
        def _():
            for i in (2 * tile, 2 * tile + 1):
                w_own[i].wait()
                w_out[i].wait_recv()

    def zero(n):
        @pl.when(n == 2)
        def _():
            acci[...] = jnp.zeros_like(acci)
            acco[...] = jnp.zeros_like(acco)

    def total(*refs):
        out = refs[0].astype(F32)
        for ref in refs[1:]:
            out = out + ref.astype(F32)
        return out

    def start(n, *copies):
        for i in copies:
            msg(n, i).start()

    def arrived(n, *copies):
        for i in copies:
            msg(n, i).wait_recv()

    def p0(n):
        weights(n, 0)
        pp[n, 0] = dot(tk[n, 0], wi[:, 0:FP]).astype(BF)
        pp[n, 1] = dot_nt(tk[n, 1], wo[0:FP, :]).astype(BF)
        start(n, 0)

    def q0(n):
        arrived(n, 27)
        for i, (j, size) in enumerate(QT):
            weights(n, 1 + i)
            pq[n, 0, :, j : j + size] = dot(tk[n, 0], wi[:, FP + j : FP + j + size]).astype(BF)
            pq[n, 1, :, j : j + size] = dot_nt(tk[n, 1], wo[FP + j : FP + j + size, :]).astype(BF)
        start(n, 13, 15, 14, 16)

    def p1(n):
        arrived(n, 0)
        s1[n] = total(pp[n, :, rows(yl, 64)], yp[n]).astype(BF)
        start(n, 1, 3, 2, 4)

    def q1a(n):
        arrived(n, 13)
        szq[n, 0] = total(pq[n, 0, rows(zr, 32)], rzq[n, 0]).astype(BF)
        start(n, 17)

    def q1b(n):
        arrived(n, 15)
        szq[n, 1] = total(pq[n, 1, rows(zl, 32)], rzq[n, 1]).astype(BF)
        start(n, 18)

    def p2a(n):
        arrived(n, 1)
        szp[n, 0] = total(s1[n, 0, rows(zr, 16)], rzp[n, 0]).astype(BF)
        start(n, 5)

    def p2b(n):
        arrived(n, 3)
        szp[n, 1] = total(s1[n, 1, rows(zl, 16)], rzp[n, 1]).astype(BF)
        start(n, 6)

    def q2(n):
        landed(rzq.at[n, pl.ds(2, 4)], rs.at[n % 4, RECV[14]])
        for t, a, b in ((0, 3, 4), (1, 2, 5)):
            for mine in (False, True):
                half = yl if mine else 1 - yl
                here = pl.ds(pl.multiple_of(z * 32 + half * 16, 16), 16)
                sums = total(pq[n, t, here], rzq[n, a, rows(half, 16)], rzq[n, b, rows(half, 16)])
                if mine:
                    kq[n, t] = sums
                else:
                    syq[n, t] = sums.astype(BF)
        start(n, 12)

    def p3(n):
        landed(rzp.at[n, pl.ds(2, 4)], rs.at[n % 4, RECV[2]])
        hidden = total(s1[n, 0, rows(z, 16)], rzp[n, 3], rzp[n, 4])
        back = total(s1[n, 1, rows(z, 16)], rzp[n, 2], rzp[n, 5])
        here = pl.ds(pl.multiple_of(yl * 64 + z * 16, 16), 16)
        gp[n, 0, here], gp[n, 1, here] = activate(hidden, back)
        start(n, 7, 8)

    def q3(n):
        arrived(n, 12)
        here = pl.ds(pl.multiple_of(z * 32 + yl * 16, 16), 16)
        gq[n, 0, here], gq[n, 1, here] = activate(total(kq[n, 0], yq[n, 0]), total(kq[n, 1], yq[n, 1]))
        start(n, 19)

    def p4a(n):
        arrived(n, 7)
        start(n, 9)

    def p4b(n):
        arrived(n, 8)
        start(n, 10)

    def q4(n):
        arrived(n, 19)
        start(n, 20, 21)

    def p5(n):
        landed(gp.at[n, :, pl.ds(pl.multiple_of(yl * 64 + z2 * 16, 16), 16)], rs.at[n % 4, RECV[9]])
        start(n, 11)

    def q5a(n):
        arrived(n, 20)
        start(n, 22)

    def q5b(n):
        arrived(n, 21)
        start(n, 23)

    def s6_wait(n):
        landed(gq.at[n, :, rows(z2, 32)], rs.at[n % 4, RECV[22]])
        arrived(n, 11)

    def cols(t, n):
        yield 0, FP, gp[n, t]
        for j, size in QT:
            yield FP + j, size, gq[n, t, :, j : j + size]

    def grads(n):
        s6_wait(n)
        for half, ref in ((oth_d, doth), (own_d, down)):
            ref[n] = dot_nt(gp[n, 1], wi[half, 0:FP]) + dot_nt(gq[n, 1], wi[half, FP:FH])
            if ref is doth:
                start(n, 24)
        tkt[...] = tk[n, 0].T
        for j, size, g in cols(1, n):
            acci[:, j : j + size] += dot(tkt[...], g)
        for j, size, a in cols(0, n):
            acco[j : j + size, :] += dot(a.T, tk[n, 1])

    def s7(n):
        arrived(n, 24)
        down[n] += dsib[n]

    def width_sums(n):
        s7(n)

        @pl.when(n >= 1)
        def _():
            start(n, 25)

    def tokens_in(n):
        @pl.when(n == 0)
        def _():
            tok_msg(7).wait_recv()
            for m in (4, 5, 6):
                tok_msg(m).start()
            start(7, 27)

        for m in range(1, 7):

            @pl.when(n == m - 1)
            def _():
                tok_msg(m).wait_recv()
                start(m, 27)

    order = (
        (p5, 5), (q0, 0), (q1a, 1), (p3, 3), (p4a, 4), (p4b, 4), (p2b, 2), (q1b, 1), (p2a, 2), (p0, 0), (q2, 2), (p1, 1),
        (q4, 4), (q5a, 5), (q5b, 5), (q3, 3), (tokens_in, 0), (zero, 0), (width_sums, 7), (grads, 6),
    )

    def step(n, _):
        for op, late in order:

            @pl.when((n >= late) & (n < N + late))
            def _():
                op(n - late)

        return 0

    lax.fori_loop(0, N + 5, step, 0)

    last = N - 1
    s7(last - 1)
    start(last - 1, 25)
    s6_wait(last)
    for half, ref in ((oth_d, doth), (own_d, down)):
        ref[last] = dot_nt(gp[last, 1], wi[half, 0:FP]) + dot_nt(gq[last, 1], wi[half, FP:FH])
        if ref is doth:
            msg(last, 24).start()
    tkt[...] = tk[last, 0].T
    outs = []
    for i, (j, size, g) in enumerate(cols(1, last)):
        there = pl.ds(pl.multiple_of(k * FH + j, 128), size)
        for mine, half in ((False, oth_d), (True, own_d)):
            sti[half, j : j + size] = (acci[half, j : j + size] + dot(tkt[half, :], g)).astype(BF)
            src, dst = sti.at[half, j : j + size], gin_ref.at[:, there]
            if mine:
                cp = pltpu.make_async_copy(src, dst, ls.at[6 + i])
            else:
                cp = rc(src, dst, os.at[i], orr.at[i], sib)
            cp.start()
            outs.append(cp)
    s7(last)
    landed(dr.at[pl.ds(4, 3)], rs25.at[1])
    yhs[...] = (down[last] + dr[4] + dr[5] + dr[6]).astype(BF)
    yh_msg = rc(yhs, yhr, hs.at[0], hr.at[0], yhp)
    yh_msg.start()
    for i, (j, size, a) in enumerate(cols(0, last)):
        there = pl.ds(pl.multiple_of(k * FH + j, 128), size)
        at = a.T
        for mine, half in ((False, oth_d), (True, own_d)):
            sto[j : j + size, half] = (acco[j : j + size, half] + dot(at, tk[last, 1, :, half])).astype(BF)
            src, dst = sto.at[j : j + size, half], gout_ref.at[there]
            if mine:
                cp = pltpu.make_async_copy(src, dst, ls.at[9 + i])
            else:
                cp = rc(src, dst, os.at[3 + i], orr.at[3 + i], sib)
            cp.start()
            outs.append(cp)
    landed(dr.at[pl.ds(1, 3)], rs25.at[0])
    yh_msg.wait()
    gtok_ref[...] = (down[0] + dr[1] + dr[2] + dr[3] + yhr[...].astype(F32)).astype(BF)
    for cp in outs:
        cp.wait()

    for n in range(N):
        landed(wo.at[pl.ds(0, 1152)], ss.at[n])
    landed(wo.at[pl.ds(0, 768)], ss.at[N])
    landed(wo.at[pl.ds(0, 896)], ss.at[N + 1])
    for cp in w_out:
        cp.wait_send()


def shards(tokens, weight_in, weight_out, upstream):
    vm = lambda *shape, dtype=BF: pltpu.VMEM(shape, dtype)
    dma = lambda *shape: pltpu.SemaphoreType.DMA(shape)
    vmem, hbm = pl.BlockSpec(memory_space=pltpu.VMEM), pl.BlockSpec(memory_space=pl.ANY)
    return pl.pallas_call(
        kernel,
        out_shape=(
            jax.ShapeDtypeStruct((TB, DH), BF),
            jax.ShapeDtypeStruct((DH, 2 * FH), BF),
            jax.ShapeDtypeStruct((2 * FH, DH), BF),
        ),
        in_specs=[vmem, hbm, hbm, vmem],
        out_specs=(vmem, hbm, hbm),
        scratch_shapes=[
            vm(DC, FH), vm(FH, DC), vm(N, 2, TB, DC),
            vm(N, 2, TB, FP), vm(N, 2, 64, FP), vm(N, 2, 64, FP), vm(N, 6, 16, FP), vm(N, 2, 16, FP), vm(N, 2, TB, FP),
            vm(N, 2, TB, FQ), vm(N, 6, 32, FQ), vm(N, 2, 32, FQ), vm(N, 2, 16, FQ, dtype=F32), vm(N, 2, 16, FQ), vm(N, 2, 16, FQ), vm(N, 2, TB, FQ),
            vm(DC, FH, dtype=F32), vm(FH, DC, dtype=F32), vm(DC, FH), vm(FH, DC),
            vm(N, TB, DH, dtype=F32), vm(N, TB, DH, dtype=F32), vm(N, TB, DH, dtype=F32), vm(N, TB, DH, dtype=F32),
            vm(TB, DH), vm(TB, DH), vm(DC, TB),
            dma(N + 2), dma(4, 17), dma(2), dma(N), dma(N), dma(12), dma(6), dma(6), dma(6), dma(6), dma(1), dma(1),
        ],
        compiler_params=pltpu.CompilerParams(
            collective_id=0, has_side_effects=True, vmem_limit_bytes=62 << 20
        ),
    )(tokens, weight_in, weight_out, upstream)


def solution(mesh):
    placed = (P("col", "row"), P("row", "col"), P("col", "row"), P("col", "row"))
    return jax.shard_map(
        shards,
        mesh=mesh,
        in_specs=placed,
        out_specs=(P("col", "row"), P("row", "col"), P("col", "row")),
        check_vma=False,
    )
```

time: 159 us -> 118 us (0.74)
  Pallas kernels: 151 us -> 111 us
    pallas_call x1, Pallas kernels: 151 us -> 111 us  [shards(): pl.pallas_call(kernel, out_shape=(jax.ShapeDtypeStruct((TB, DH), BF), jax...]
where the time goes in v2:
time: 118 us
  Pallas kernels  111 us (94%)
  local copies, waits for them, and re-layouts  6.32 us (5%)
    pallas_call x1, Pallas kernels, shards(): pl.pallas_call(kernel, out_shape=(jax.ShapeDtypeStruct((TB, DH), BF), jax...  111 us
    unnamed x5, local copies, waits for them, and re-layouts  6.32 us

profile of v2, /device:TPU:0, one launch (start us, length us, event | category | flops | bytes accessed | tf_op | source)
XLA Modules:
  0.0 117.8 jit_solution(9291453885147464155)
XLA Ops:
  0.6 110.8 %shard_map.67 = (bf16[128,384]{1,0:T(8,128)(2,1)}, bf16[384,3072]{1,0:T(8,128)(2,1)}, bf16[3072,384]{1,0:T(8,128)(2,1)}) custom-call(bf16[128,384]{1,0:T(8,128)(2,1)} %tok_ref.1, bf16[384,3072]{1,0:T(8,128)(2,1)} %win_ref.1, bf16[3072,384]{1,0:T(8,128)(2,1)} %wout_ref.1, bf16[128,384]{1,0:T(8,128)(2,1)} %up_ref.1), custom_call_target="tpu_custom_call" | custom-call | tf_op jit(solution)/shard_map/pallas_call | solution.py:434
  111.5 1.5 %copy.10 = bf16[128,384]{1,0:T(8,128)(2,1)} copy(bf16[128,384]{1,0:T(8,128)(2,1)} %get-tuple-element.6) | data formatting | bytes 196608
  113.0 0.0 copy-start
  113.0 3.4 %copy.11 = bf16[384,3072]{1,0:T(8,128)(2,1)} copy(bf16[384,3072]{1,0:T(8,128)(2,1)} %get-tuple-element.7) | data formatting | bytes 4718592
  116.4 0.0 copy-done
  116.4 1.4 %copy.12 = bf16[3072,384]{1,0:T(8,128)(2,1)} copy(bf16[3072,384]{1,0:T(8,128)(2,1)S(1)} %copy-done) | data formatting | bytes 4718592
Async XLA Ops:
  113.0 3.4 %copy-start = (bf16[3072,384]{1,0:T(8,128)(2,1)S(1)}, bf16[3072,384]{1,0:T(8,128)(2,1)}, u32[]{:S(2)}) copy-start(bf16[3072,384]{1,0:T(8,128)(2,1)} %get-tuple-element.8) | copy-start | bytes 7077892

commit v3 on v2

--- a/solution.py
+++ b/solution.py
@@ -19,7 +19,7 @@
 FP = 640
 FQ = 896
 RECV = {0: 0, 1: 1, 3: 2, 2: 3, 4: 3, 5: 3, 6: 3, 7: 4, 8: 5, 9: 6, 10: 6, 11: 7}
-RECV |= {13: 8, 15: 9, 14: 10, 16: 10, 17: 10, 18: 10, 12: 11, 19: 12, 20: 13, 21: 14, 22: 15, 23: 15, 24: 16}
+RECV |= {13: 8, 15: 9, 14: 10, 16: 10, 17: 10, 18: 10, 12: 11, 19: 12, 20: 13, 21: 14, 22: 15, 23: 15, 24: 16, 28: 17}
 QT = ((0, 512), (512, FQ - 512))
 TILES = ((0, FP),) + tuple((FP + j, size) for j, size in QT)
 
@@ -47,7 +47,7 @@
 def kernel(
     tok_ref, win_ref, wout_ref, up_ref,
     gtok_ref, gin_ref, gout_ref,
-    wi, wo, tk, pp, yp, s1, rzp, szp, gp, pq, rzq, szq, kq, syq, yq, gq,
+    wi, wo, tk, ppf, ppo, pp, yp, s1, rzp, szp, gp, pq, rzq, szq, kq, syq, yq, gq,
     acci, acco, sti, sto, down, doth, dsib, dr, yhs, yhr, tkt,
     ss, rs, rs25, rs26, rs27, ls, ws, wr, os, orr, hs, hr,
 ):
@@ -85,7 +85,7 @@
         right_p = pl.ds(pl.multiple_of(yl * 64 + zr * 16, 16), 16)
         own_q = pl.ds(pl.multiple_of(z * 32 + yl * 16, 16), 16)
         if i == 0:
-            src, dst, dev = pp.at[n, :, rows(1 - yl, 64)], yp.at[n], ypart
+            src, dst, dev = pp.at[n], yp.at[n], ypart
         elif i == 1:
             src, dst, dev = s1.at[n, 0, rows(z2, 16)], rzp.at[n, 0], right
         elif i == 2:
@@ -108,7 +108,10 @@
             src = dst = gp.at[n, 1, right_p]
             dev = left
         elif i == 11:
-            src = dst = gp.at[n, :, rows(yl, 64)]
+            src = dst = gp.at[n, 1, rows(yl, 64)]
+            dev = ypart
+        elif i == 28:
+            src = dst = gp.at[n, 0, rows(yl, 64)]
             dev = ypart
         elif i == 12:
             src, dst, dev = syq.at[n], yq.at[n], ypart
@@ -150,7 +153,7 @@
         elif i == 25:
             recv = rs25.at[(n - 1) // 3]
         else:
-            recv = rs.at[n % 4, RECV[i]]
+            recv = rs.at[n, RECV[i]]
         return rc(src, dst, ss.at[N if i == 25 else n], recv, dev)
 
     own_d = pl.ds(pl.multiple_of(k * DH, DH), DH)
@@ -162,6 +165,11 @@
         dev = {1: xl, 2: xr, 3: xx, 4: xx, 5: xl, 6: xr, 7: yhp}[m]
         src = tk.at[0 if m in (1, 2, 3, 7) else 7, :, :, own_d]
         return rc(src, tk.at[m, :, :, own_d], ss.at[N + 1], rs26.at[m], dev)
+
+    barrier = pltpu.get_barrier_semaphore()
+    partners = (sib, ypart, right, left, yhp, xr, xl, xx)
+    for dev in partners:
+        pl.semaphore_signal(barrier, inc=1, device_id=dev, device_id_type=MESH)
 
     w_own, w_out = [], []
     for i, (j, size) in enumerate(TILES):
@@ -176,24 +184,25 @@
             rc(win_ref.at[:, other], wi.at[own_d, here], ws.at[2 * i], wr.at[2 * i], sib),
             rc(wout_ref.at[other], wo.at[here, own_d], ws.at[2 * i + 1], wr.at[2 * i + 1], sib),
         ]
-    w_order = [2, 3, 4, 5, 0, 1]
+    w_order = range(6)
     for i in w_order:
         w_own[i].start()
-    tk[0, 0, :, own_d] = tok_ref[...]
-    tk[0, 1, :, own_d] = up_ref[...]
-
-    barrier = pltpu.get_barrier_semaphore()
-    partners = (sib, ypart, right, left, yhp, xr, xl, xx)
-    for dev in partners:
-        pl.semaphore_signal(barrier, inc=1, device_id=dev, device_id_type=MESH)
+    t_own = [
+        pltpu.make_async_copy(ref, tk.at[0, i, :, own_d], ls.at[12 + i])
+        for i, ref in enumerate((tok_ref, up_ref))
+    ]
+    for cp in t_own:
+        cp.start()
     pl.semaphore_wait(barrier, len(partners))
+    for cp in t_own:
+        cp.wait()
 
     msg(0, 27).start()
     tok_msg(7).start()
     for i in w_order:
         w_out[i].start()
-    for m in (1, 2, 3):
-        tok_msg(m).start()
+    tok_msg(1).start()
+    tok_msg(2).start()
 
     def weights(n, tile):
         @pl.when(n == 0)
@@ -223,13 +232,15 @@
             msg(n, i).wait_recv()
 
     def p0(n):
+        arrived(n, 27)
         weights(n, 0)
-        pp[n, 0] = dot(tk[n, 0], wi[:, 0:FP]).astype(BF)
-        pp[n, 1] = dot_nt(tk[n, 1], wo[0:FP, :]).astype(BF)
+        ppf[0] = dot(tk[n, 0], wi[:, 0:FP])
+        ppf[1] = dot_nt(tk[n, 1], wo[0:FP, :])
+        pp[n] = ppf[:, rows(1 - yl, 64)].astype(BF)
         start(n, 0)
+        ppo[n] = ppf[:, rows(yl, 64)]
 
     def q0(n):
-        arrived(n, 27)
         for i, (j, size) in enumerate(QT):
             weights(n, 1 + i)
             pq[n, 0, :, j : j + size] = dot(tk[n, 0], wi[:, FP + j : FP + j + size]).astype(BF)
@@ -238,7 +249,7 @@
 
     def p1(n):
         arrived(n, 0)
-        s1[n] = total(pp[n, :, rows(yl, 64)], yp[n]).astype(BF)
+        s1[n] = total(ppo[n], yp[n]).astype(BF)
         start(n, 1, 3, 2, 4)
 
     def q1a(n):
@@ -253,16 +264,16 @@
 
     def p2a(n):
         arrived(n, 1)
-        szp[n, 0] = total(s1[n, 0, rows(zr, 16)], rzp[n, 0]).astype(BF)
+        szp[n, 0] = total(ppo[n, 0, rows(zr, 16)], yp[n, 0, rows(zr, 16)], rzp[n, 0]).astype(BF)
         start(n, 5)
 
     def p2b(n):
         arrived(n, 3)
-        szp[n, 1] = total(s1[n, 1, rows(zl, 16)], rzp[n, 1]).astype(BF)
+        szp[n, 1] = total(ppo[n, 1, rows(zl, 16)], yp[n, 1, rows(zl, 16)], rzp[n, 1]).astype(BF)
         start(n, 6)
 
     def q2(n):
-        landed(rzq.at[n, pl.ds(2, 4)], rs.at[n % 4, RECV[14]])
+        landed(rzq.at[n, pl.ds(2, 4)], rs.at[n, RECV[14]])
         for t, a, b in ((0, 3, 4), (1, 2, 5)):
             for mine in (False, True):
                 half = yl if mine else 1 - yl
@@ -275,9 +286,9 @@
         start(n, 12)
 
     def p3(n):
-        landed(rzp.at[n, pl.ds(2, 4)], rs.at[n % 4, RECV[2]])
-        hidden = total(s1[n, 0, rows(z, 16)], rzp[n, 3], rzp[n, 4])
-        back = total(s1[n, 1, rows(z, 16)], rzp[n, 2], rzp[n, 5])
+        landed(rzp.at[n, pl.ds(2, 4)], rs.at[n, RECV[2]])
+        hidden = total(ppo[n, 0, rows(z, 16)], yp[n, 0, rows(z, 16)], rzp[n, 3], rzp[n, 4])
+        back = total(ppo[n, 1, rows(z, 16)], yp[n, 1, rows(z, 16)], rzp[n, 2], rzp[n, 5])
         here = pl.ds(pl.multiple_of(yl * 64 + z * 16, 16), 16)
         gp[n, 0, here], gp[n, 1, here] = activate(hidden, back)
         start(n, 7, 8)
@@ -301,8 +312,8 @@
         start(n, 20, 21)
 
     def p5(n):
-        landed(gp.at[n, :, pl.ds(pl.multiple_of(yl * 64 + z2 * 16, 16), 16)], rs.at[n % 4, RECV[9]])
-        start(n, 11)
+        landed(gp.at[n, :, pl.ds(pl.multiple_of(yl * 64 + z2 * 16, 16), 16)], rs.at[n, RECV[9]])
+        start(n, 11, 28)
 
     def q5a(n):
         arrived(n, 20)
@@ -311,10 +322,6 @@
     def q5b(n):
         arrived(n, 21)
         start(n, 23)
-
-    def s6_wait(n):
-        landed(gq.at[n, :, rows(z2, 32)], rs.at[n % 4, RECV[22]])
-        arrived(n, 11)
 
     def cols(t, n):
         yield 0, FP, gp[n, t]
@@ -322,7 +329,8 @@
             yield FP + j, size, gq[n, t, :, j : j + size]
 
     def grads(n):
-        s6_wait(n)
+        landed(gq.at[n, :, rows(z2, 32)], rs.at[n, RECV[22]])
+        arrived(n, 11, 28)
         for half, ref in ((oth_d, doth), (own_d, down)):
             ref[n] = dot_nt(gp[n, 1], wi[half, 0:FP]) + dot_nt(gq[n, 1], wi[half, FP:FH])
             if ref is doth:
@@ -347,6 +355,7 @@
     def tokens_in(n):
         @pl.when(n == 0)
         def _():
+            tok_msg(3).start()
             tok_msg(7).wait_recv()
             for m in (4, 5, 6):
                 tok_msg(m).start()
@@ -360,8 +369,8 @@
                 start(m, 27)
 
     order = (
-        (p5, 5), (q0, 0), (q1a, 1), (p3, 3), (p4a, 4), (p4b, 4), (p2b, 2), (q1b, 1), (p2a, 2), (p0, 0), (q2, 2), (p1, 1),
-        (q4, 4), (q5a, 5), (q5b, 5), (q3, 3), (tokens_in, 0), (zero, 0), (width_sums, 7), (grads, 6),
+        (p0, 0), (q0, 0), (q1b, 1), (q2, 3), (p1, 2), (p4a, 5), (p3, 4), (p4b, 5), (p2b, 3),
+        (q1a, 1), (q3, 4), (tokens_in, 0), (p2a, 3), (p5, 6), (q4, 5), (zero, 0), (width_sums, 9), (grads, 8), (q5a, 6), (q5b, 6),
     )
 
     def step(n, _):
@@ -373,46 +382,54 @@
 
         return 0
 
-    lax.fori_loop(0, N + 5, step, 0)
+    lax.fori_loop(0, N + 7, step, 0)
 
     last = N - 1
+    outs = []
+
+    def give(src, dst, i):
+        outs.append(rc(src, dst, os.at[i], orr.at[i], sib))
+        outs[-1].start()
+
+    def in_tile(i):
+        j, size = TILES[i]
+        g = gp[last, 1] if i == 0 else gq[last, 1, :, j - FP : j - FP + size]
+        there = pl.ds(pl.multiple_of(k * FH + j, 128), size)
+        sti[:, j : j + size] = (acci[oth_d, j : j + size] + dot(tkt[oth_d, :], g)).astype(BF)
+        give(sti.at[:, j : j + size], gin_ref.at[:, there], i)
+        gin_ref[:, there] = (acci[own_d, j : j + size] + dot(tkt[own_d, :], g)).astype(BF)
+
+    def out_tile(i):
+        j, size = TILES[i]
+        a = gp[last, 0] if i == 0 else gq[last, 0, :, j - FP : j - FP + size]
+        there = pl.ds(pl.multiple_of(k * FH + j, 128), size)
+        at = a.T
+        sto[j : j + size] = (acco[j : j + size, oth_d] + dot(at, tk[last, 1, :, oth_d])).astype(BF)
+        give(sto.at[j : j + size], gout_ref.at[there], 3 + i)
+        gout_ref[there] = (acco[j : j + size, own_d] + dot(at, tk[last, 1, :, own_d])).astype(BF)
+
     s7(last - 1)
     start(last - 1, 25)
-    s6_wait(last)
+    tkt[...] = tk[last, 0].T
+    landed(gq.at[last, :, rows(z2, 32)], rs.at[last, RECV[22]])
     for half, ref in ((oth_d, doth), (own_d, down)):
-        ref[last] = dot_nt(gp[last, 1], wi[half, 0:FP]) + dot_nt(gq[last, 1], wi[half, FP:FH])
+        ref[last] = dot_nt(gq[last, 1], wi[half, FP:FH])
+    for i in (1, 2):
+        in_tile(i)
+        out_tile(i)
+    arrived(last, 11)
+    for half, ref in ((oth_d, doth), (own_d, down)):
+        ref[last] += dot_nt(gp[last, 1], wi[half, 0:FP])
         if ref is doth:
-            msg(last, 24).start()
-    tkt[...] = tk[last, 0].T
-    outs = []
-    for i, (j, size, g) in enumerate(cols(1, last)):
-        there = pl.ds(pl.multiple_of(k * FH + j, 128), size)
-        for mine, half in ((False, oth_d), (True, own_d)):
-            sti[half, j : j + size] = (acci[half, j : j + size] + dot(tkt[half, :], g)).astype(BF)
-            src, dst = sti.at[half, j : j + size], gin_ref.at[:, there]
-            if mine:
-                cp = pltpu.make_async_copy(src, dst, ls.at[6 + i])
-            else:
-                cp = rc(src, dst, os.at[i], orr.at[i], sib)
-            cp.start()
-            outs.append(cp)
+            start(last, 24)
+    in_tile(0)
     s7(last)
     landed(dr.at[pl.ds(4, 3)], rs25.at[1])
     yhs[...] = (down[last] + dr[4] + dr[5] + dr[6]).astype(BF)
     yh_msg = rc(yhs, yhr, hs.at[0], hr.at[0], yhp)
     yh_msg.start()
-    for i, (j, size, a) in enumerate(cols(0, last)):
-        there = pl.ds(pl.multiple_of(k * FH + j, 128), size)
-        at = a.T
-        for mine, half in ((False, oth_d), (True, own_d)):
-            sto[j : j + size, half] = (acco[j : j + size, half] + dot(at, tk[last, 1, :, half])).astype(BF)
-            src, dst = sto.at[j : j + size, half], gout_ref.at[there]
-            if mine:
-                cp = pltpu.make_async_copy(src, dst, ls.at[9 + i])
-            else:
-                cp = rc(src, dst, os.at[3 + i], orr.at[3 + i], sib)
-            cp.start()
-            outs.append(cp)
+    arrived(last, 28)
+    out_tile(0)
     landed(dr.at[pl.ds(1, 3)], rs25.at[0])
     yh_msg.wait()
     gtok_ref[...] = (down[0] + dr[1] + dr[2] + dr[3] + yhr[...].astype(F32)).astype(BF)
@@ -427,32 +444,51 @@
         cp.wait_send()
 
 
+def hand_on(gtok, gin, gout, gtok_out, gin_out, gout_out, sem):
+    copies = [
+        pltpu.make_async_copy(a, b, sem.at[i])
+        for i, (a, b) in enumerate(((gin, gin_out), (gout, gout_out), (gtok, gtok_out)))
+    ]
+    for cp in copies:
+        cp.start()
+    for cp in copies:
+        cp.wait()
+
+
 def shards(tokens, weight_in, weight_out, upstream):
     vm = lambda *shape, dtype=BF: pltpu.VMEM(shape, dtype)
     dma = lambda *shape: pltpu.SemaphoreType.DMA(shape)
     vmem, hbm = pl.BlockSpec(memory_space=pltpu.VMEM), pl.BlockSpec(memory_space=pl.ANY)
-    return pl.pallas_call(
+    results = pl.pallas_call(
         kernel,
         out_shape=(
-            jax.ShapeDtypeStruct((TB, DH), BF),
-            jax.ShapeDtypeStruct((DH, 2 * FH), BF),
-            jax.ShapeDtypeStruct((2 * FH, DH), BF),
+            vm(TB, DH),
+            vm(DH, 2 * FH),
+            vm(2 * FH, DH),
         ),
-        in_specs=[vmem, hbm, hbm, vmem],
-        out_specs=(vmem, hbm, hbm),
+        in_specs=[hbm] * 4,
+        out_specs=(vmem, vmem, vmem),
         scratch_shapes=[
             vm(DC, FH), vm(FH, DC), vm(N, 2, TB, DC),
-            vm(N, 2, TB, FP), vm(N, 2, 64, FP), vm(N, 2, 64, FP), vm(N, 6, 16, FP), vm(N, 2, 16, FP), vm(N, 2, TB, FP),
+            vm(2, TB, FP, dtype=F32), vm(N, 2, 64, FP, dtype=F32), vm(N, 2, 64, FP), vm(N, 2, 64, FP), vm(N, 2, 64, FP), vm(N, 6, 16, FP), vm(N, 2, 16, FP), vm(N, 2, TB, FP),
             vm(N, 2, TB, FQ), vm(N, 6, 32, FQ), vm(N, 2, 32, FQ), vm(N, 2, 16, FQ, dtype=F32), vm(N, 2, 16, FQ), vm(N, 2, 16, FQ), vm(N, 2, TB, FQ),
-            vm(DC, FH, dtype=F32), vm(FH, DC, dtype=F32), vm(DC, FH), vm(FH, DC),
+            vm(DC, FH, dtype=F32), vm(FH, DC, dtype=F32), vm(DH, FH), vm(FH, DH),
             vm(N, TB, DH, dtype=F32), vm(N, TB, DH, dtype=F32), vm(N, TB, DH, dtype=F32), vm(N, TB, DH, dtype=F32),
             vm(TB, DH), vm(TB, DH), vm(DC, TB),
-            dma(N + 2), dma(4, 17), dma(2), dma(N), dma(N), dma(12), dma(6), dma(6), dma(6), dma(6), dma(1), dma(1),
+            dma(N + 2), dma(N, 18), dma(2), dma(N), dma(N), dma(14), dma(6), dma(6), dma(6), dma(6), dma(1), dma(1),
         ],
         compiler_params=pltpu.CompilerParams(
-            collective_id=0, has_side_effects=True, vmem_limit_bytes=62 << 20
+            collective_id=0, has_side_effects=True, vmem_limit_bytes=53 << 20
         ),
     )(tokens, weight_in, weight_out, upstream)
+    return pl.pallas_call(
+        hand_on,
+        out_shape=tuple(jax.ShapeDtypeStruct(a.shape, a.dtype) for a in results),
+        in_specs=[vmem] * 3,
+        out_specs=(hbm,) * 3,
+        scratch_shapes=[dma(3)],
+        compiler_params=pltpu.CompilerParams(vmem_limit_bytes=1 << 20),
+    )(*(pltpu.with_memory_space_constraint(a, pltpu.VMEM) for a in results))
 
 
 def solution(mesh):

time: 118 us -> 113 us (0.958)
  local copies, waits for them, and re-layouts: 6.32 us -> 0 us
    unnamed x5 -> x0, local copies, waits for them, and re-layouts: 6.32 us -> none
    pallas_call x1 -> x2, Pallas kernels: 111 us -> 112 us  [the longest x1 110 us: shards(): pl.pallas_call(kernel, out_shape=(vm(TB, DH), vm(DH, 2 * FH), vm(2 * FH,...]
where the time goes in v3:
time: 113 us
  Pallas kernels  112 us (99%)
    pallas_call x1, Pallas kernels, shards(): pl.pallas_call(kernel, out_shape=(vm(TB, DH), vm(DH, 2 * FH), vm(2 * FH,...  110 us

profile of v3, /device:TPU:0, one launch (start us, length us, event | category | flops | bytes accessed | tf_op | source)
XLA Modules:
  0.0 112.6 jit_solution(1526670360583229794)
XLA Ops:
  0.6 109.7 %shard_map.67 = (bf16[128,384]{1,0:T(8,128)(2,1)S(1)}, bf16[384,3072]{1,0:T(8,128)(2,1)S(1)}, bf16[3072,384]{1,0:T(8,128)(2,1)S(1)}) custom-call(bf16[128,384]{1,0:T(8,128)(2,1)} %tok_ref.1, bf16[384,3072]{1,0:T(8,128)(2,1)} %win_ref.1, bf16[3072,384]{1,0:T(8,128)(2,1)} %wout_ref.1, bf16[128,384]{1,0:T(8,128)(2,1)} %up_ref.1), custom_call_target="tpu_custom_call" | custom-call | tf_op jit(solution)/shard_map/pallas_call | solution.py:462
  110.3 2.2 %shard_map.68 = (bf16[128,384]{1,0:T(8,128)(2,1)}, bf16[384,3072]{1,0:T(8,128)(2,1)}, bf16[3072,384]{1,0:T(8,128)(2,1)}) custom-call(bf16[128,384]{1,0:T(8,128)(2,1)S(1)} %get-tuple-element.6.gtok, bf16[384,3072]{1,0:T(8,128)(2,1)S(1)} %get-tuple-element.7.gin, bf16[3072,384]{1,0:T(8,128)(2,1)S(1)} %get-tuple-element.8.gout), custom_call_target="tpu_custom_call" | custom-call | tf_op jit(solution)/shard_map/pallas_call | solution.py:484

commit v4 on v3

--- a/solution.py
+++ b/solution.py
@@ -141,30 +141,46 @@
             dev = left
         elif i == 24:
             src, dst, dev = doth.at[n], dsib.at[n], sib
-        elif i == 25:
-            m, later = (n - 1) % 3, (n - 1) // 3
-            dx = (1 - later) * (1 + 2 * m - 3 * (m // 2)) + later * (2 - m + 3 * (m // 2))
-            src, dst, dev = down.at[n], dr.at[n], at_col(yh, (x + dx) % 4)
         elif i == 27:
             src = dst = tk.at[n, :, :, own_d]
             dev = sib
         if i == 27:
             recv = rs27.at[n]
-        elif i == 25:
-            recv = rs25.at[(n - 1) // 3]
         else:
             recv = rs.at[n, RECV[i]]
-        return rc(src, dst, ss.at[N if i == 25 else n], recv, dev)
+        return rc(src, dst, ss.at[n], recv, dev)
 
     own_d = pl.ds(pl.multiple_of(k * DH, DH), DH)
     oth_d = pl.ds(pl.multiple_of((1 - k) * DH, DH), DH)
     own_f = pl.ds(pl.multiple_of(k * FH, FH), FH)
     oth_f = pl.ds(pl.multiple_of((1 - k) * FH, FH), FH)
 
-    def tok_msg(m):
-        dev = {1: xl, 2: xr, 3: xx, 4: xx, 5: xl, 6: xr, 7: yhp}[m]
-        src = tk.at[0 if m in (1, 2, 3, 7) else 7, :, :, own_d]
-        return rc(src, tk.at[m, :, :, own_d], ss.at[N + 1], rs26.at[m], dev)
+    top, bottom = pl.ds(0, 64), pl.ds(64, 64)
+
+    def tok_msgs(m):
+        if m in (1, 2):
+            src = tk.at[0, :, (top, bottom)[m - 1], own_d]
+            parts = ((src, tk.at[m, :, top, own_d], xl), (src, tk.at[m, :, bottom, own_d], xr))
+        else:
+            dev = {3: xx, 4: xx, 5: xl, 6: xr, 7: yhp}[m]
+            parts = ((tk.at[0 if m in (3, 7) else 7, :, :, own_d], tk.at[m, :, :, own_d], dev),)
+        return [rc(src, dst, ss.at[N + 1], rs26.at[m], dev) for src, dst, dev in parts]
+
+    def send_tokens(m):
+        for cp in tok_msgs(m):
+            cp.start()
+
+    def tokens_landed(m):
+        landed(tk.at[m, :, :, own_d], rs26.at[m])
+
+    def send_width(m):
+        if m in (1, 2):
+            there = (top, bottom)[m - 1]
+            parts = ((down.at[m, top], dr.at[1, there], xr), (down.at[m, bottom], dr.at[2, there], xl))
+        else:
+            parts = ((down.at[m], dr.at[m], {3: xx, 4: xx, 5: xr, 6: xl}[m]),)
+        for src, dst, dev in parts:
+            rc(src, dst, ss.at[N], rs25.at[(m - 1) // 3], dev).start()
 
     barrier = pltpu.get_barrier_semaphore()
     partners = (sib, ypart, right, left, yhp, xr, xl, xx)
@@ -184,7 +200,7 @@
             rc(win_ref.at[:, other], wi.at[own_d, here], ws.at[2 * i], wr.at[2 * i], sib),
             rc(wout_ref.at[other], wo.at[here, own_d], ws.at[2 * i + 1], wr.at[2 * i + 1], sib),
         ]
-    w_order = range(6)
+    w_order = (2, 3, 4, 5, 0, 1)
     for i in w_order:
         w_own[i].start()
     t_own = [
@@ -198,11 +214,11 @@
         cp.wait()
 
     msg(0, 27).start()
-    tok_msg(7).start()
+    send_tokens(1)
+    send_tokens(7)
     for i in w_order:
         w_out[i].start()
-    tok_msg(1).start()
-    tok_msg(2).start()
+    send_tokens(2)
 
     def weights(n, tile):
         @pl.when(n == 0)
@@ -232,7 +248,6 @@
             msg(n, i).wait_recv()
 
     def p0(n):
-        arrived(n, 27)
         weights(n, 0)
         ppf[0] = dot(tk[n, 0], wi[:, 0:FP])
         ppf[1] = dot_nt(tk[n, 1], wo[0:FP, :])
@@ -241,6 +256,7 @@
         ppo[n] = ppf[:, rows(yl, 64)]
 
     def q0(n):
+        arrived(n, 27)
         for i, (j, size) in enumerate(QT):
             weights(n, 1 + i)
             pq[n, 0, :, j : j + size] = dot(tk[n, 0], wi[:, FP + j : FP + j + size]).astype(BF)
@@ -347,29 +363,29 @@
 
     def width_sums(n):
         s7(n)
-
-        @pl.when(n >= 1)
-        def _():
-            start(n, 25)
+        for m in range(1, 6):
+
+            @pl.when(n == m)
+            def _():
+                send_width(m)
 
     def tokens_in(n):
-        @pl.when(n == 0)
-        def _():
-            tok_msg(3).start()
-            tok_msg(7).wait_recv()
-            for m in (4, 5, 6):
-                tok_msg(m).start()
-            start(7, 27)
-
         for m in range(1, 7):
 
             @pl.when(n == m - 1)
             def _():
-                tok_msg(m).wait_recv()
+                tokens_landed(m)
                 start(m, 27)
+                if m == 1:
+                    send_tokens(3)
+                if m == 2:
+                    tokens_landed(7)
+                    for far in (4, 5, 6):
+                        send_tokens(far)
+                    start(7, 27)
 
     order = (
-        (p0, 0), (q0, 0), (q1b, 1), (q2, 3), (p1, 2), (p4a, 5), (p3, 4), (p4b, 5), (p2b, 3),
+        (q0, 0), (p0, 0), (q1b, 1), (q2, 3), (p1, 2), (p4a, 5), (p3, 4), (p4b, 5), (p2b, 3),
         (q1a, 1), (q3, 4), (tokens_in, 0), (p2a, 3), (p5, 6), (q4, 5), (zero, 0), (width_sums, 9), (grads, 8), (q5a, 6), (q5b, 6),
     )
 
@@ -409,7 +425,7 @@
         gout_ref[there] = (acco[j : j + size, own_d] + dot(at, tk[last, 1, :, own_d])).astype(BF)
 
     s7(last - 1)
-    start(last - 1, 25)
+    send_width(last - 1)
     tkt[...] = tk[last, 0].T
     landed(gq.at[last, :, rows(z2, 32)], rs.at[last, RECV[22]])
     for half, ref in ((oth_d, doth), (own_d, down)):

time: 113 us -> 111 us (0.982)
  Pallas kernels: 112 us -> 110 us
    pallas_call x1, Pallas kernels: 110 us -> 108 us  [shards(): pl.pallas_call(kernel, out_shape=(vm(TB, DH), vm(DH, 2 * FH), vm(2 * FH,...]
where the time goes in v4:
time: 111 us
  Pallas kernels  110 us (99%)
    pallas_call x1, Pallas kernels, shards(): pl.pallas_call(kernel, out_shape=(vm(TB, DH), vm(DH, 2 * FH), vm(2 * FH,...  108 us
    pallas_call x1, Pallas kernels, shards(): pl.pallas_call(hand_on, out_shape=tuple((jax.ShapeDtypeStruct(a.shape, a....  2.22 us

profile of v4, /device:TPU:0, one launch (start us, length us, event | category | flops | bytes accessed | tf_op | source)
XLA Modules:
  0.0 110.7 jit_solution(3320768240384493972)
XLA Ops:
  0.6 107.8 %shard_map.67 = (bf16[128,384]{1,0:T(8,128)(2,1)S(1)}, bf16[384,3072]{1,0:T(8,128)(2,1)S(1)}, bf16[3072,384]{1,0:T(8,128)(2,1)S(1)}) custom-call(bf16[128,384]{1,0:T(8,128)(2,1)} %tok_ref.1, bf16[384,3072]{1,0:T(8,128)(2,1)} %win_ref.1, bf16[3072,384]{1,0:T(8,128)(2,1)} %wout_ref.1, bf16[128,384]{1,0:T(8,128)(2,1)} %up_ref.1), custom_call_target="tpu_custom_call" | custom-call | tf_op jit(solution)/shard_map/pallas_call | solution.py:478
  108.5 2.2 %shard_map.68 = (bf16[128,384]{1,0:T(8,128)(2,1)}, bf16[384,3072]{1,0:T(8,128)(2,1)}, bf16[3072,384]{1,0:T(8,128)(2,1)}) custom-call(bf16[128,384]{1,0:T(8,128)(2,1)S(1)} %get-tuple-element.6.gtok, bf16[384,3072]{1,0:T(8,128)(2,1)S(1)} %get-tuple-element.7.gin, bf16[3072,384]{1,0:T(8,128)(2,1)S(1)} %get-tuple-element.8.gout), custom_call_target="tpu_custom_call" | custom-call | tf_op jit(solution)/shard_map/pallas_call | solution.py:500

commit v5 on v4

--- a/solution.py
+++ b/solution.py
@@ -19,7 +19,7 @@
 FP = 640
 FQ = 896
 RECV = {0: 0, 1: 1, 3: 2, 2: 3, 4: 3, 5: 3, 6: 3, 7: 4, 8: 5, 9: 6, 10: 6, 11: 7}
-RECV |= {13: 8, 15: 9, 14: 10, 16: 10, 17: 10, 18: 10, 12: 11, 19: 12, 20: 13, 21: 14, 22: 15, 23: 15, 24: 16, 28: 17}
+RECV |= {13: 8, 15: 9, 14: 10, 16: 10, 17: 10, 18: 10, 12: 11, 19: 12, 20: 13, 21: 14, 22: 15, 23: 15, 24: 16, 28: 17, 29: 15, 30: 15, 31: 6, 32: 6}
 QT = ((0, 512), (512, FQ - 512))
 TILES = ((0, FP),) + tuple((FP + j, size) for j, size in QT)
 
@@ -98,9 +98,9 @@
             src, dst, dev = szp.at[n, 0], rzp.at[n, 4], right
         elif i == 6:
             src, dst, dev = szp.at[n, 1], rzp.at[n, 5], left
-        elif i in (7, 8):
-            src = dst = gp.at[n, :, own_p]
-            dev = right if i == 7 else left
+        elif i in (7, 8, 31, 32):
+            src = dst = gp.at[n, 0 if i in (7, 32) else 1, own_p]
+            dev = right if i in (7, 31) else left
         elif i == 9:
             src = dst = gp.at[n, 0, left_p]
             dev = right
@@ -130,9 +130,9 @@
         elif i == 19:
             src = dst = gq.at[n, :, own_q]
             dev = ypart
-        elif i in (20, 21):
-            src = dst = gq.at[n, :, rows(z, 32)]
-            dev = right if i == 20 else left
+        elif i in (20, 21, 29, 30):
+            src = dst = gq.at[n, 0 if i in (20, 30) else 1, rows(z, 32)]
+            dev = right if i in (20, 29) else left
         elif i == 22:
             src = dst = gq.at[n, 0, rows(zl, 32)]
             dev = right
@@ -147,7 +147,7 @@
         if i == 27:
             recv = rs27.at[n]
         else:
-            recv = rs.at[n, RECV[i]]
+            recv = rs.at[n % 6, RECV[i]]
         return rc(src, dst, ss.at[n], recv, dev)
 
     own_d = pl.ds(pl.multiple_of(k * DH, DH), DH)
@@ -289,7 +289,7 @@
         start(n, 6)
 
     def q2(n):
-        landed(rzq.at[n, pl.ds(2, 4)], rs.at[n, RECV[14]])
+        landed(rzq.at[n, pl.ds(2, 4)], rs.at[n % 6, RECV[14]])
         for t, a, b in ((0, 3, 4), (1, 2, 5)):
             for mine in (False, True):
                 half = yl if mine else 1 - yl
@@ -302,12 +302,12 @@
         start(n, 12)
 
     def p3(n):
-        landed(rzp.at[n, pl.ds(2, 4)], rs.at[n, RECV[2]])
+        landed(rzp.at[n, pl.ds(2, 4)], rs.at[n % 6, RECV[2]])
         hidden = total(ppo[n, 0, rows(z, 16)], yp[n, 0, rows(z, 16)], rzp[n, 3], rzp[n, 4])
         back = total(ppo[n, 1, rows(z, 16)], yp[n, 1, rows(z, 16)], rzp[n, 2], rzp[n, 5])
         here = pl.ds(pl.multiple_of(yl * 64 + z * 16, 16), 16)
         gp[n, 0, here], gp[n, 1, here] = activate(hidden, back)
-        start(n, 7, 8)
+        start(n, 7, 8, 31, 32)
 
     def q3(n):
         arrived(n, 12)
@@ -325,10 +325,10 @@
 
     def q4(n):
         arrived(n, 19)
-        start(n, 20, 21)
+        start(n, 20, 21, 29, 30)
 
     def p5(n):
-        landed(gp.at[n, :, pl.ds(pl.multiple_of(yl * 64 + z2 * 16, 16), 16)], rs.at[n, RECV[9]])
+        landed(rzp.at[n, pl.ds(0, 4)], rs.at[n % 6, RECV[9]])
         start(n, 11, 28)
 
     def q5a(n):
@@ -345,7 +345,7 @@
             yield FP + j, size, gq[n, t, :, j : j + size]
 
     def grads(n):
-        landed(gq.at[n, :, rows(z2, 32)], rs.at[n, RECV[22]])
+        landed(rzq.at[n, pl.ds(0, 4)], rs.at[n % 6, RECV[22]])
         arrived(n, 11, 28)
         for half, ref in ((oth_d, doth), (own_d, down)):
             ref[n] = dot_nt(gp[n, 1], wi[half, 0:FP]) + dot_nt(gq[n, 1], wi[half, FP:FH])
@@ -386,7 +386,7 @@
 
     order = (
         (q0, 0), (p0, 0), (q1b, 1), (q2, 3), (p1, 2), (p4a, 5), (p3, 4), (p4b, 5), (p2b, 3),
-        (q1a, 1), (q3, 4), (tokens_in, 0), (p2a, 3), (p5, 6), (q4, 5), (zero, 0), (width_sums, 9), (grads, 8), (q5a, 6), (q5b, 6),
+        (q1a, 1), (q3, 4), (tokens_in, 0), (p2a, 3), (p5, 6), (q4, 5), (q5a, 6), (q5b, 6), (zero, 0), (width_sums, 8), (grads, 7),
     )
 
     def step(n, _):
@@ -398,7 +398,7 @@
 
         return 0
 
-    lax.fori_loop(0, N + 7, step, 0)
+    lax.fori_loop(0, N + 6, step, 0)
 
     last = N - 1
     outs = []
@@ -427,23 +427,24 @@
     s7(last - 1)
     send_width(last - 1)
     tkt[...] = tk[last, 0].T
-    landed(gq.at[last, :, rows(z2, 32)], rs.at[last, RECV[22]])
+    landed(rzq.at[last, pl.ds(0, 4)], rs.at[last % 6, RECV[22]])
     for half, ref in ((oth_d, doth), (own_d, down)):
         ref[last] = dot_nt(gq[last, 1], wi[half, FP:FH])
-    for i in (1, 2):
-        in_tile(i)
-        out_tile(i)
     arrived(last, 11)
     for half, ref in ((oth_d, doth), (own_d, down)):
         ref[last] += dot_nt(gp[last, 1], wi[half, 0:FP])
         if ref is doth:
             start(last, 24)
-    in_tile(0)
+    in_tile(1)
     s7(last)
     landed(dr.at[pl.ds(4, 3)], rs25.at[1])
     yhs[...] = (down[last] + dr[4] + dr[5] + dr[6]).astype(BF)
     yh_msg = rc(yhs, yhr, hs.at[0], hr.at[0], yhp)
     yh_msg.start()
+    in_tile(2)
+    in_tile(0)
+    out_tile(1)
+    out_tile(2)
     arrived(last, 28)
     out_tile(0)
     landed(dr.at[pl.ds(1, 3)], rs25.at[0])
@@ -491,7 +492,7 @@
             vm(DC, FH, dtype=F32), vm(FH, DC, dtype=F32), vm(DH, FH), vm(FH, DH),
             vm(N, TB, DH, dtype=F32), vm(N, TB, DH, dtype=F32), vm(N, TB, DH, dtype=F32), vm(N, TB, DH, dtype=F32),
             vm(TB, DH), vm(TB, DH), vm(DC, TB),
-            dma(N + 2), dma(N, 18), dma(2), dma(N), dma(N), dma(14), dma(6), dma(6), dma(6), dma(6), dma(1), dma(1),
+            dma(N + 2), dma(6, 18), dma(2), dma(N), dma(N), dma(14), dma(6), dma(6), dma(6), dma(6), dma(1), dma(1),
         ],
         compiler_params=pltpu.CompilerParams(
             collective_id=0, has_side_effects=True, vmem_limit_bytes=53 << 20

time: 111 us -> 111 us (level)
  no operation moved by 1% of the time
where the time goes in v5:
time: 111 us; the launch traced here: 110 us
  Pallas kernels  110 us (99%)
    pallas_call x1, Pallas kernels, shards(): pl.pallas_call(kernel, out_shape=(vm(TB, DH), vm(DH, 2 * FH), vm(2 * FH,...  108 us
    pallas_call x1, Pallas kernels, shards(): pl.pallas_call(hand_on, out_shape=tuple((jax.ShapeDtypeStruct(a.shape, a....  2.22 us

profile of v5, /device:TPU:0, one launch (start us, length us, event | category | flops | bytes accessed | tf_op | source)
XLA Modules:
  0.0 110.4 jit_solution(10408331357607653756)
XLA Ops:
  0.6 107.6 %shard_map.67 = (bf16[128,384]{1,0:T(8,128)(2,1)S(1)}, bf16[384,3072]{1,0:T(8,128)(2,1)S(1)}, bf16[3072,384]{1,0:T(8,128)(2,1)S(1)}) custom-call(bf16[128,384]{1,0:T(8,128)(2,1)} %tok_ref.1, bf16[384,3072]{1,0:T(8,128)(2,1)} %win_ref.1, bf16[3072,384]{1,0:T(8,128)(2,1)} %wout_ref.1, bf16[128,384]{1,0:T(8,128)(2,1)} %up_ref.1), custom_call_target="tpu_custom_call" | custom-call | tf_op jit(solution)/shard_map/pallas_call | solution.py:479
  108.2 2.2 %shard_map.68 = (bf16[128,384]{1,0:T(8,128)(2,1)}, bf16[384,3072]{1,0:T(8,128)(2,1)}, bf16[3072,384]{1,0:T(8,128)(2,1)}) custom-call(bf16[128,384]{1,0:T(8,128)(2,1)S(1)} %get-tuple-element.6.gtok, bf16[384,3072]{1,0:T(8,128)(2,1)S(1)} %get-tuple-element.7.gin, bf16[3072,384]{1,0:T(8,128)(2,1)S(1)} %get-tuple-element.8.gout), custom_call_target="tpu_custom_call" | custom-call | tf_op jit(solution)/shard_map/pallas_call | solution.py:501
